TPU v7x, 32 devices: a whole 2x2x4 slice. The times are simulated.
32 devices in a mesh: slab: 8 (over z, y), chan: 4 (over x, core).
Axes of the slice: x: 2, y: 2, z: 4, core: 2. Of those that a mesh axis runs over, the one named last changes fastest.
Arguments:
- features: bfloat16 [4, 32, 128, 512], P(None, 'slab', 'chan'), may hold values from -6 to 6
- neighbours: int32 [32, 27], P('slab'), may hold values from -1 to 7, as said below
- face_lists: int32 [8, 2, 2], P('slab'), may hold values from -1 to 3, as said below
- weight_first: bfloat16 [27, 128, 128], P(None, None, 'chan'), may hold values from -0.109375 to 0.109375
- bias_first: float32 [128], P('chan'), may hold values from -3 to 3
- weight_second: bfloat16 [27, 128, 128], P(None, None, 'chan'), may hold values from -0.109375 to 0.109375
- bias_second: float32 [128], P('chan'), may hold values from -3 to 3
- level_embed: float32 [4, 128], P(None, 'chan'), may hold values from -3 to 3
Outputs:
- denoised: bfloat16 [4, 32, 128, 512], P(None, 'slab', 'chan')
Inputs may be any that keep to these rules, and one draw needn't show every extreme that they name: `neighbours`: slab s holds in its used slots, in some order, the active bricks of its two brick layers at positions of a 8 x 8 grid; each layer has at most 2 active bricks. Rows of unused slots are all -1; a used slot names itself at offset 13. Offsets with dz = -1 from the bottom layer name the slab below (never for slab 0), dz = +1 from the top layer the slab above (never for the last slab). `face_lists`: entry [s, 0, c] is the slot of the active bottom-layer brick at position c, entry [s, 1, c] that of the top-layer brick; -1 where the position has no active brick. The slots of a slab's used bricks each appear once.
All inputs are finite; a program needn't handle non-finite values.
Results may differ from a plain program's by a relative error of at most 0.02.
Values may be sent and summed in bfloat16 or wider, within the bound.
A program may use at most 128 MiB of HBM per device.

v0:
```python
import jax
import jax.numpy as jnp
import numpy as np
from jax import lax
from jax.sharding import PartitionSpec as P


def shifted(value, axis, steps):
    count = lax.axis_size(axis)
    first, last = (max(0, -steps), min(count, count - steps))
    return lax.ppermute(value, axis, [(source, source + steps) for source in range(first, last)])


def position_tables():
    place = np.arange(1000)
    pos_z = place // 100
    pos_y = place // 10 % 10
    pos_x = place % 10
    step_z = np.where(pos_z == 0, -1, np.where(pos_z == 9, 1, 0))
    step_y = np.where(pos_y == 0, -1, np.where(pos_y == 9, 1, 0))
    step_x = np.where(pos_x == 0, -1, np.where(pos_x == 9, 1, 0))
    vox_z = (pos_z - 1) % 8
    vox_y = (pos_y - 1) % 8
    vox_x = (pos_x - 1) % 8
    offset_k = 9 * (step_z + 1) + 3 * (step_y + 1) + (step_x + 1)
    within = 64 * vox_z + 8 * vox_y + vox_x
    flat_plane = 8 * vox_y + vox_x
    side = np.where(
        step_z < 0,
        1,
        np.where(
            step_z > 0,
            0,
            np.where(step_y < 0, 3, np.where(step_y > 0, 2, np.where(step_x < 0, 5, 4))),
        ),
    )
    side_off = np.where(
        step_z != 0, 8 * vox_y + vox_x, np.where(step_y != 0, 8 * vox_z + vox_x, 8 * vox_z + vox_y)
    )
    center_pos = (step_z == 0) & (step_y == 0) & (step_x == 0)
    return (
        offset_k.astype(np.int32),
        step_z.astype(np.int32),
        within.astype(np.int32),
        flat_plane.astype(np.int32),
        (side * 64 + side_off).astype(np.int32),
        center_pos,
    )


def fetch(bricks, listed):
    count = bricks.shape[1]
    with_blank = jnp.concatenate([bricks, jnp.zeros_like(bricks[:, :1])], axis=1)
    return jnp.take(with_blank, jnp.where(listed < 0, count, listed), axis=1)


def crop(result):
    count, outputs = (result.shape[0], result.shape[1])
    result = jnp.pad(result, ((0, 0), (0, 0), (0, 22)))
    return result.reshape(count, outputs, 8, 10, 10)[:, :, :, :8, :8].reshape(count, outputs, 512)


def shifted_products(kernel, level_rows):
    offsets = [
        100 * dz + 10 * dy + dx for dz in (-1, 0, 1) for dy in (-1, 0, 1) for dx in (-1, 0, 1)
    ]
    acc = jnp.zeros((level_rows.shape[1], kernel.shape[1], 778), jnp.float32)
    for k in range(27):
        window = level_rows[:, :, 111 + offsets[k] : 889 + offsets[k]]
        acc = acc + jnp.einsum("oc,cbq->boq", kernel[k], window, preferred_element_type=jnp.float32)
    return acc


def conv_layer(features, table, face_lists, weight, bias, shift):
    levels, count, group, voxels = features.shape
    face = face_lists.shape[2]
    offset_k, step_z, within, flat_plane, side_code, center_pos = position_tables()
    upward = fetch(features, face_lists[0, 1])
    downward = fetch(features, face_lists[0, 0])
    below = shifted(upward, "slab", 1)[:, :, :, 448:512]
    above = shifted(downward, "slab", -1)[:, :, :, 0:64]
    flat = features.transpose(0, 2, 1, 3).reshape(levels, group, count * 512)
    below_flat = below.transpose(0, 2, 1, 3).reshape(levels, group, face * 64)
    above_flat = above.transpose(0, 2, 1, 3).reshape(levels, group, face * 64)
    blank = jnp.zeros((levels, group, 1), features.dtype)
    pool = jnp.concatenate([flat, below_flat, above_flat, blank], axis=2)
    target = jnp.take(table, jnp.asarray(offset_k), axis=1)
    dz_row = jnp.asarray(step_z)[None, :]
    in_slab = (target >= 0) & (target < count)
    from_below = (dz_row < 0) & (target >= count) & (target < count + face)
    from_above = (dz_row > 0) & (target >= count + face)
    zero_at = count * 512 + 2 * face * 64
    index = jnp.where(
        in_slab,
        target * 512 + jnp.asarray(within)[None, :],
        jnp.where(
            from_below | from_above,
            count * 512 + (target - count) * 64 + jnp.asarray(flat_plane)[None, :],
            zero_at,
        ),
    )
    padded = jnp.take(pool, index.reshape(-1), axis=2).reshape(levels, group, count, 1000)

    def per_level(level_rows):
        return crop(shifted_products(weight, level_rows))

    term = lax.map(per_level, padded)
    whole = lax.psum(term.astype(jnp.bfloat16), "chan").astype(jnp.float32)
    total = lax.dynamic_slice_in_dim(whole, lax.axis_index("chan") * group, group, 2)
    mask = (table[:, 13] >= 0).astype(jnp.float32)
    act = (
        jax.nn.silu(total + bias[None, None, :, None] + shift[:, None, :, None])
        * mask[None, :, None, None]
    )
    return act.astype(jnp.bfloat16)


def shards(
    features,
    neighbours,
    face_lists,
    weight_first,
    bias_first,
    weight_second,
    bias_second,
    level_embed,
):
    hidden = conv_layer(features, neighbours, face_lists, weight_first, bias_first, level_embed)
    no_shift = jnp.zeros_like(level_embed)
    return conv_layer(hidden, neighbours, face_lists, weight_second, bias_second, no_shift)


def solution(mesh):
    placed = (
        P(None, "slab", "chan", None),
        P("slab", None),
        P("slab", None, None),
        P(None, None, "chan"),
        P("chan"),
        P(None, None, "chan"),
        P("chan"),
        P(None, "chan"),
    )
    return jax.shard_map(
        shards, mesh=mesh, in_specs=placed, out_specs=P(None, "slab", "chan", None), check_vma=False
    )
```

profile of v0, /device:TPU:0, one launch (start us, length us, event | category | flops | bytes accessed | tf_op | source)
XLA Modules:
  0.0 687.3 jit_solution(17632924214651010011)
XLA Ops:
  9.2 4.9 collective-permute-start
  16.2 2.9 gather_fusion.2
  19.6 5.7 collective-permute-done
  25.8 2.5 copy.67
  28.3 28.4 %gather_fusion.3 = bf16[4000,4,32]{2,1,0:T(4,128)(2,1)} fusion(bf16[4,32,2305]{1,0,2:T(4,128)(2,1)S(1)} %copy.67, s32[4096]{0:T(1024)S(1)} %pad_clamp_fusion), kind=kCustom, calls=%fused_computation.2.clone | custom fusion | bytes 2064000 | tf_op jit(solution)/shard_map/jit(_take)/gather | solution.py:102
  56.7 16.6 %broadcast_select_fusion = bf16[4000,4,32]{2,1,0:T(4,128)(2,1)} fusion(bf16[4000,4,32]{2,1,0:T(4,128)(2,1)} %gather_fusion.3, pred[4000]{0:T(1024)(128)(4,1)S(1)} %compare_and_fusion), kind=kLoop, calls=%fused_computation.245 | loop fusion | flops 512000 | bytes 2052000 | tf_op jit(solution)/shard_map/jit(_take)/select_n | solution.py:102
  73.3 6.7 copy.69
  81.5 208.5 %while.24 = (s32[]{:T(128)}, bf16[4,4,128,512]{3,2,1,0:T(8,128)(2,1)}, bf16[4,32,4,1000]{3,1,2,0:T(8,128)(2,1)}, bf16[27,128,32]{1,2,0:T(8,128)(2,1)S(1)}, s32[]{:T(128)}, /*index=5*/bf16[]{:T(256)}) while((s32[]{:T(128)}, bf16[4,4,128,512]{3,2,1,0:T(8,128)(2,1)}, bf16[4,32,4,1000]{3,1,2,0:T(8,128)(2,1)}, bf16[27,128,32]{1,2,0:T(8,128)(2,1)S(1)}, ...), condition=%wide.region_1.5_spmd, body=%wide.region_0.4_spmd.sunk | while | flops 699079680 | bytes 97006152 | solution.py:107
  87.4 1.7 fusion.447
  90.9 1.8 fusion.449
  101.2 1.7 fusion.455
  104.6 1.7 fusion.457
  108.0 1.8 fusion.459
  113.2 1.8 fusion.462
  119.9 11.7 %bitcast_add_fusion.23 = bf16[4,128,778]{1,2,0:T(8,128)(2,1)S(1)} fusion(f32[4,778,128]{2,1,0:T(8,128)S(1)} %fusion.440, f32[4,778,128]{2,1,0:T(8,128)S(1)} %fusion.441, f32[4,778,128]{2,1,0:T(8,128)S(1)} %fusion.442, f32[4,778,128]{2,1,0:T(8,128)S(1)} %fusion.443, f32[4,778,128]{2,1,0:T(8,128)S(1)} %fusion.444, f32[4,778,128]{2,1,0:T(8,128)S(1)} %fusion.445, ...), kind=kOutput, calls=%fused_computation.7.clone.1 | convolution fusion | flops 36248576 | bytes 42534912 | tf_op jit(solution)/shard_map/while/body/eval_jaxpr/oc,cbq->boq/dot_general | solution.py:70
  139.5 1.7 fusion.447
  143.0 1.8 fusion.449
  153.3 1.7 fusion.455
  160.1 1.8 fusion.459
  165.3 1.8 fusion.462
  172.0 11.7 %bitcast_add_fusion.23 = bf16[4,128,778]{1,2,0:T(8,128)(2,1)S(1)} fusion(f32[4,778,128]{2,1,0:T(8,128)S(1)} %fusion.440, f32[4,778,128]{2,1,0:T(8,128)S(1)} %fusion.441, f32[4,778,128]{2,1,0:T(8,128)S(1)} %fusion.442, f32[4,778,128]{2,1,0:T(8,128)S(1)} %fusion.443, f32[4,778,128]{2,1,0:T(8,128)S(1)} %fusion.444, f32[4,778,128]{2,1,0:T(8,128)S(1)} %fusion.445, ...), kind=kOutput, calls=%fused_computation.7.clone.1 | convolution fusion | flops 36248576 | bytes 42534912 | tf_op jit(solution)/shard_map/while/body/eval_jaxpr/oc,cbq->boq/dot_general | solution.py:70
  191.7 1.7 fusion.447
  195.1 1.8 fusion.449
  205.4 1.7 fusion.455
  212.2 1.8 fusion.459
  217.4 1.8 fusion.462
  224.1 11.7 %bitcast_add_fusion.23 = bf16[4,128,778]{1,2,0:T(8,128)(2,1)S(1)} fusion(f32[4,778,128]{2,1,0:T(8,128)S(1)} %fusion.440, f32[4,778,128]{2,1,0:T(8,128)S(1)} %fusion.441, f32[4,778,128]{2,1,0:T(8,128)S(1)} %fusion.442, f32[4,778,128]{2,1,0:T(8,128)S(1)} %fusion.443, f32[4,778,128]{2,1,0:T(8,128)S(1)} %fusion.444, f32[4,778,128]{2,1,0:T(8,128)S(1)} %fusion.445, ...), kind=kOutput, calls=%fused_computation.7.clone.1 | convolution fusion | flops 36248576 | bytes 42534912 | tf_op jit(solution)/shard_map/while/body/eval_jaxpr/oc,cbq->boq/dot_general | solution.py:70
  243.8 1.7 fusion.447
  247.2 1.8 fusion.449
  257.5 1.7 fusion.455
  261.0 1.7 fusion.457
  264.4 1.8 fusion.459
  269.6 1.8 fusion.462
  276.3 11.7 %bitcast_add_fusion.23 = bf16[4,128,778]{1,2,0:T(8,128)(2,1)S(1)} fusion(f32[4,778,128]{2,1,0:T(8,128)S(1)} %fusion.440, f32[4,778,128]{2,1,0:T(8,128)S(1)} %fusion.441, f32[4,778,128]{2,1,0:T(8,128)S(1)} %fusion.442, f32[4,778,128]{2,1,0:T(8,128)S(1)} %fusion.443, f32[4,778,128]{2,1,0:T(8,128)S(1)} %fusion.444, f32[4,778,128]{2,1,0:T(8,128)S(1)} %fusion.445, ...), kind=kOutput, calls=%fused_computation.7.clone.1 | convolution fusion | flops 36248576 | bytes 42534912 | tf_op jit(solution)/shard_map/while/body/eval_jaxpr/oc,cbq->boq/dot_general | solution.py:70
  290.3 53.2 %all-reduce.7.cloned.1.call-done = bf16[4,4,128,512]{3,2,1,0:T(8,128)(2,1)} async-done(((bf16[4,4,128,512]{3,2,1,0:T(8,128)(2,1)}), bf16[4,4,128,512]{3,2,1,0:T(8,128)(2,1)}) %all-reduce.7.cloned.1.call-update) | async-done | bytes 2097168 | tf_op jit(solution)/shard_map/psum | solution.py:108
  346.3 3.4 collective-permute-start.2
  352.7 8.1 %collective-permute-done.2 = bf16[4,2,32,512]{3,2,0,1:T(8,128)(2,1)S(1)} collective-permute-done((bf16[4,2,32,512]{3,2,0,1:T(8,128)(2,1)S(1)}, bf16[4,2,32,512]{3,2,0,1:T(8,128)(2,1)S(1)}, u32[]{:S(2)}, u32[]{:S(2)}) %collective-permute-start.2) | collective-permute-done | bytes 262176 | tf_op jit(solution)/shard_map/ppermute | solution.py:11
  361.4 2.5 copy.74
  363.9 28.6 %gather_fusion.6 = bf16[4000,4,32]{2,1,0:T(4,128)(2,1)} fusion(bf16[4,32,2305]{1,0,2:T(4,128)(2,1)S(1)} %copy.74, s32[4096]{0:T(1024)S(1)} %pad_clamp_fusion), kind=kCustom, calls=%fused_computation.6.clone | custom fusion | bytes 2064000 | tf_op jit(solution)/shard_map/jit(_take)/gather | solution.py:102
  392.5 16.6 %broadcast_select_fusion.1 = bf16[4000,4,32]{2,1,0:T(4,128)(2,1)} fusion(bf16[4000,4,32]{2,1,0:T(4,128)(2,1)} %gather_fusion.6, pred[4000]{0:T(1024)(128)(4,1)S(1)} %compare_and_fusion), kind=kLoop, calls=%fused_computation.246 | loop fusion | flops 512000 | bytes 2052000 | tf_op jit(solution)/shard_map/jit(_take)/select_n | solution.py:102
  409.1 6.7 copy.76
  417.3 208.5 %while.25 = (s32[]{:T(128)}, bf16[4,4,128,512]{3,2,1,0:T(8,128)(2,1)}, bf16[4,32,4,1000]{3,1,2,0:T(8,128)(2,1)}, bf16[27,128,32]{1,2,0:T(8,128)(2,1)S(1)}, s32[]{:T(128)}, /*index=5*/bf16[]{:T(256)}) while((s32[]{:T(128)}, bf16[4,4,128,512]{3,2,1,0:T(8,128)(2,1)}, bf16[4,32,4,1000]{3,1,2,0:T(8,128)(2,1)}, bf16[27,128,32]{1,2,0:T(8,128)(2,1)S(1)}, ...), condition=%wide.region_4.8_spmd, body=%wide.region_3.7_spmd.sunk | while | flops 699079680 | bytes 97006152 | solution.py:107
  423.2 1.7 fusion.527
  426.6 1.8 fusion.529
  443.7 1.8 fusion.539
  448.9 1.8 fusion.542
  455.7 11.7 %bitcast_add_fusion.24 = bf16[4,128,778]{1,2,0:T(8,128)(2,1)S(1)} fusion(f32[4,778,128]{2,1,0:T(8,128)S(1)} %fusion.520, f32[4,778,128]{2,1,0:T(8,128)S(1)} %fusion.521, f32[4,778,128]{2,1,0:T(8,128)S(1)} %fusion.522, f32[4,778,128]{2,1,0:T(8,128)S(1)} %fusion.523, f32[4,778,128]{2,1,0:T(8,128)S(1)} %fusion.524, f32[4,778,128]{2,1,0:T(8,128)S(1)} %fusion.525, ...), kind=kOutput, calls=%fused_computation.126.clone.1 | convolution fusion | flops 36248576 | bytes 42534912 | tf_op jit(solution)/shard_map/while/body/eval_jaxpr/oc,cbq->boq/dot_general | solution.py:70
  475.3 1.7 fusion.527
  478.7 1.8 fusion.529
  495.8 1.8 fusion.539
  501.0 1.8 fusion.542
  507.8 11.7 %bitcast_add_fusion.24 = bf16[4,128,778]{1,2,0:T(8,128)(2,1)S(1)} fusion(f32[4,778,128]{2,1,0:T(8,128)S(1)} %fusion.520, f32[4,778,128]{2,1,0:T(8,128)S(1)} %fusion.521, f32[4,778,128]{2,1,0:T(8,128)S(1)} %fusion.522, f32[4,778,128]{2,1,0:T(8,128)S(1)} %fusion.523, f32[4,778,128]{2,1,0:T(8,128)S(1)} %fusion.524, f32[4,778,128]{2,1,0:T(8,128)S(1)} %fusion.525, ...), kind=kOutput, calls=%fused_computation.126.clone.1 | convolution fusion | flops 36248576 | bytes 42534912 | tf_op jit(solution)/shard_map/while/body/eval_jaxpr/oc,cbq->boq/dot_general | solution.py:70
  527.4 1.7 fusion.527
  530.8 1.8 fusion.529
  548.0 1.8 fusion.539
  553.2 1.8 fusion.542
  559.9 11.7 %bitcast_add_fusion.24 = bf16[4,128,778]{1,2,0:T(8,128)(2,1)S(1)} fusion(f32[4,778,128]{2,1,0:T(8,128)S(1)} %fusion.520, f32[4,778,128]{2,1,0:T(8,128)S(1)} %fusion.521, f32[4,778,128]{2,1,0:T(8,128)S(1)} %fusion.522, f32[4,778,128]{2,1,0:T(8,128)S(1)} %fusion.523, f32[4,778,128]{2,1,0:T(8,128)S(1)} %fusion.524, f32[4,778,128]{2,1,0:T(8,128)S(1)} %fusion.525, ...), kind=kOutput, calls=%fused_computation.126.clone.1 | convolution fusion | flops 36248576 | bytes 42534912 | tf_op jit(solution)/shard_map/while/body/eval_jaxpr/oc,cbq->boq/dot_general | solution.py:70
  579.5 1.7 fusion.527
  583.0 1.8 fusion.529
  600.1 1.8 fusion.539
  605.3 1.8 fusion.542
  612.0 11.7 %bitcast_add_fusion.24 = bf16[4,128,778]{1,2,0:T(8,128)(2,1)S(1)} fusion(f32[4,778,128]{2,1,0:T(8,128)S(1)} %fusion.520, f32[4,778,128]{2,1,0:T(8,128)S(1)} %fusion.521, f32[4,778,128]{2,1,0:T(8,128)S(1)} %fusion.522, f32[4,778,128]{2,1,0:T(8,128)S(1)} %fusion.523, f32[4,778,128]{2,1,0:T(8,128)S(1)} %fusion.524, f32[4,778,128]{2,1,0:T(8,128)S(1)} %fusion.525, ...), kind=kOutput, calls=%fused_computation.126.clone.1 | convolution fusion | flops 36248576 | bytes 42534912 | tf_op jit(solution)/shard_map/while/body/eval_jaxpr/oc,cbq->boq/dot_general | solution.py:70
  625.8 52.5 %all-reduce.9.cloned.1.call-done = bf16[4,4,128,512]{3,2,1,0:T(8,128)(2,1)} async-done(((bf16[4,4,128,512]{3,2,1,0:T(8,128)(2,1)}), bf16[4,4,128,512]{3,2,1,0:T(8,128)(2,1)}) %all-reduce.9.cloned.1.call-update) | async-done | bytes 2097168 | tf_op jit(solution)/shard_map/psum | solution.py:108
  678.2 2.2 multiply_convert_fusion
  (293 shorter events, 270.5 us)
Async XLA Ops:
  6.5 336.9 %all-reduce.7.cloned.1.call-start = ((), (), s32[]{:S(2)}) async-start(), calls=%async_computation | async-start | bytes 4194304 | tf_op jit(solution)/shard_map/psum | solution.py:108
  7.3 8.8 %copy-start.4 = (s32[4,27]{1,0:T(4,128)S(1)}, s32[4,27]{1,0:T(4,128)}, u32[]{:S(2)}) copy-start(s32[4,27]{1,0:T(4,128)} %param.27) | copy-start | bytes 1300
  7.3 8.9 %copy-start.5 = (s32[1000]{0:T(1024)S(1)}, s32[1000]{0:T(1024)}, u32[]{:S(2)}) copy-start(s32[1000]{0:T(1024)} %constant.145) | copy-start | bytes 12004
  8.4 10.8 %copy-start.6 = (s32[1000]{0:T(1024)S(1)}, s32[1000]{0:T(1024)}, u32[]{:S(2)}) copy-start(s32[1000]{0:T(1024)} %constant.121.clone) | copy-start | bytes 12004
  8.5 10.8 %copy-start.7 = (s32[1000]{0:T(1024)S(1)}, s32[1000]{0:T(1024)}, u32[]{:S(2)}) copy-start(s32[1000]{0:T(1024)} %constant.122.clone) | copy-start | bytes 12004
  8.5 10.8 %copy-start.9 = (pred[1000]{0:T(1024)(128)(4,1)S(1)}, pred[1000]{0:T(1024)(128)(4,1)}, u32[]{:S(2)}) copy-start(pred[1000]{0:T(1024)(128)(4,1)} %constant.134) | copy-start | bytes 3004
  8.5 10.8 %copy-start.10 = (pred[1000]{0:T(1024)(128)(4,1)S(1)}, pred[1000]{0:T(1024)(128)(4,1)}, u32[]{:S(2)}) copy-start(pred[1000]{0:T(1024)(128)(4,1)} %constant.135) | copy-start | bytes 3004
  8.5 11.0 %copy-start.2 = (bf16[4,4,32,512]{3,2,1,0:T(8,128)(2,1)S(1)}, bf16[4,4,32,512]{3,2,1,0:T(8,128)(2,1)}, u32[]{:S(2)}) copy-start(bf16[4,4,32,512]{3,2,1,0:T(8,128)(2,1)} %param.26) | copy-start | bytes 1572868
  9.2 16.0 %collective-permute-start = (bf16[4,2,32,512]{3,2,0,1:T(8,128)(2,1)S(1)}, bf16[4,2,32,512]{3,2,0,1:T(8,128)(2,1)S(1)}, u32[]{:S(2)}, u32[]{:S(2)}) collective-permute-start(bf16[4,2,32,512]{3,2,0,1:T(8,128)(2,1)S(1)} %select_bitcast_fusion.3), channel_id=1, source_target_pairs={{0,4},{4,8},{8,12},{12,16},{16,20},{20,24},{24,28},{1,5},{5,9},{9,... | collective-permute-start | bytes 786440 | tf_op jit(solution)/shard_map/ppermute | solution.py:11
  14.8 10.7 %collective-permute-start.1 = (bf16[4,2,32,512]{3,2,0,1:T(8,128)(2,1)S(1)}, bf16[4,2,32,512]{3,2,0,1:T(8,128)(2,1)S(1)}, u32[]{:S(2)}, u32[]{:S(2)}) collective-permute-start(bf16[4,2,32,512]{3,2,0,1:T(8,128)(2,1)S(1)} %select_bitcast_fusion.2), channel_id=1, source_target_pairs={{4,0},{8,4},{12,8},{16,12},{20,16},{24,20},{28,24},{5,1},{9,5},{13... | collective-permute-start | bytes 786440 | tf_op jit(solution)/shard_map/ppermute | solution.py:11
  80.0 1.6 copy-start
  290.0 53.4 %copy-start.3 = (f32[4,32]{1,0:T(4,128)S(1)}, f32[4,32]{1,0:T(4,128)}, u32[]{:S(2)}) copy-start(f32[4,32]{1,0:T(4,128)} %param.33) | copy-start | bytes 1540
  290.0 53.4 %copy-start.8 = (f32[32]{0:T(128)S(1)}, f32[32]{0:T(128)}, u32[]{:S(2)}) copy-start(f32[32]{0:T(128)} %param.30) | copy-start | bytes 388
  290.1 388.2 %all-reduce.9.cloned.1.call-start = ((), (), s32[]{:S(2)}) async-start(), calls=%async_computation.1 | async-start | bytes 4194304 | tf_op jit(solution)/shard_map/psum | solution.py:108
  346.3 14.5 %collective-permute-start.2 = (bf16[4,2,32,512]{3,2,0,1:T(8,128)(2,1)S(1)}, bf16[4,2,32,512]{3,2,0,1:T(8,128)(2,1)S(1)}, u32[]{:S(2)}, u32[]{:S(2)}) collective-permute-start(bf16[4,2,32,512]{3,2,0,1:T(8,128)(2,1)S(1)} %select_bitcast_fusion.1), channel_id=1, source_target_pairs={{0,4},{4,8},{8,12},{12,16},{16,20},{20,24},{24,28},{1,5},{5,9},{9,... | collective-permute-start | bytes 786440 | tf_op jit(solution)/shard_map/ppermute | solution.py:11
  349.8 11.3 %collective-permute-start.3 = (bf16[4,2,32,512]{3,2,0,1:T(8,128)(2,1)S(1)}, bf16[4,2,32,512]{3,2,0,1:T(8,128)(2,1)S(1)}, u32[]{:S(2)}, u32[]{:S(2)}) collective-permute-start(bf16[4,2,32,512]{3,2,0,1:T(8,128)(2,1)S(1)} %select_bitcast_fusion), channel_id=1, source_target_pairs={{4,0},{8,4},{12,8},{16,12},{20,16},{24,20},{28,24},{5,1},{9,5},{13... | collective-permute-start | bytes 786440 | tf_op jit(solution)/shard_map/ppermute | solution.py:11
  415.8 1.5 copy-start.1
  625.8 52.5 %copy-start.11 = (f32[32]{0:T(128)S(1)}, f32[32]{0:T(128)}, u32[]{:S(2)}) copy-start(f32[32]{0:T(128)} %param.32) | copy-start | bytes 388
Sparse Core Ops, SparseCore 0:
  290.2 53.2 all-reduce.6
  625.9 52.2 all-reduce.8
where the time goes:
time: 688 us; the launch traced here: 687 us
  matrix products  393 us (57%)
  waiting for transfers between devices  119 us (17%)
  local copies, waits for them, and re-layouts  110 us (16%)
  other arithmetic  40 us (6%)
  between operations  13.8 us (2%)
  starting transfers between devices  10.9 us (2%)
    dot_general x216, matrix products, shifted_products(): jnp.einsum('oc,cbq->boq', kernel[k], window, preferred_element_type=jnp.f...  393 us
    psum x2, waiting for transfers between devices, conv_layer(): whole = lax.psum(term.astype(jnp.bfloat16), 'chan').astype(jnp.float32)  106 us
    gather x2, local copies, waits for them, and re-layouts, conv_layer(): jnp.take(pool, index.reshape(-1), axis=2)  57.1 us
    select_n x3, other arithmetic, conv_layer(): jnp.take(pool, index.reshape(-1), axis=2)  33.1 us
    ppermute x4, waiting for transfers between devices, shifted(): lax.ppermute(value, axis, [(source, source + steps) for source in range(f...  13.8 us
  transfers between devices with their start and end apart: 6, of which 4 were waited for; matrix products, arithmetic and copies ran while one was open for 1% of the time, Pallas kernels for 0%

commit v1 on v0

v1 whole, which is shorter than its diff:
```python
import functools

import jax
import jax.numpy as jnp
from jax import lax
from jax.experimental import pallas as pl
from jax.experimental.pallas import tpu as pltpu
from jax.sharding import PartitionSpec as P

MESH = pl.DeviceIdType.MESH
EDGE = 8
PLANE = EDGE * EDGE
PARTS = 3


def kernel(
    slabs,
    feat, table, faces, small, wa, wb,
    out,
    xt, w_all, small_all, pool, even, odd, face_out, face_in, staged,
    feat_send, feat_recv, w_send, w_recv, small_send, small_recv,
    face_send, face_recv, out_send, out_recv, local_sem,
):
    levels, bricks, group, voxels = feat.shape
    face = faces.shape[1]
    channels = xt.shape[1]
    blank = bricks * EDGE + 2 * face
    s, g = lax.axis_index("slab"), lax.axis_index("chan")
    chip, core = g // 2, g % 2
    across = 2 * (1 - chip) + core
    diagonal = 2 * (1 - chip) + (1 - core)
    twin = 2 * chip + (1 - core)
    peers = (across, diagonal, twin)
    has_below, has_above = s > 0, s < slabs - 1

    barrier = pltpu.get_barrier_semaphore()
    for peer in peers:
        pl.semaphore_signal(barrier, inc=1, device_id=(s, peer), device_id_type=MESH)

    @pl.when(has_below)
    def _():
        pl.semaphore_signal(barrier, inc=1, device_id=(s - 1, g), device_id_type=MESH)

    @pl.when(has_above)
    def _():
        pl.semaphore_signal(barrier, inc=1, device_id=(s + 1, g), device_id_type=MESH)

    sides = (s + slabs - 1) // slabs + (2 * slabs - 2 - s) // slabs
    pl.semaphore_wait(barrier, len(peers) + sides)

    def rows(owner):
        return pl.ds(pl.multiple_of(owner * group, group), group)

    def remote(src, dst, send, recv, peer):
        return pltpu.make_async_remote_copy(
            src_ref=src, dst_ref=dst, send_sem=send, recv_sem=recv,
            device_id=peer, device_id_type=MESH,
        )

    def feat_copy(j):
        return remote(
            feat.at[peers[j]], xt.at[:, rows(g), :], feat_send.at[j], feat_recv.at[j],
            (s, peers[j]),
        )

    per = 27 // PARTS

    def w_own(layer, part, j):
        taps = pl.ds(part * per, per)
        source = (wa, wb)[layer]
        return remote(
            source.at[taps], w_all.at[layer, taps, rows(g), :],
            w_send.at[layer, part, j], w_recv.at[layer, part, j],
            (s, (across, twin)[j]),
        )

    def w_forward(layer, part):
        taps = pl.ds(part * per, per)
        block = w_all.at[layer, taps, rows(across), :]
        return remote(
            block, block, w_send.at[layer, part, 2], w_recv.at[layer, part, 2], (s, twin)
        )

    def small_copy(j):
        return remote(
            small, small_all.at[g], small_send.at[j], small_recv.at[j], (s, peers[j])
        )

    for j in range(3):
        feat_copy(j).start()
    for j in range(3):
        small_copy(j).start()
    for part in range(PARTS):
        for j in range(2):
            w_own(0, part, j).start()
    for part in range(PARTS):
        for j in range(2):
            w_own(1, part, j).start()
    own_feat = pltpu.make_async_copy(feat.at[g], xt.at[:, rows(g), :], local_sem.at[0])
    own_wa = pltpu.make_async_copy(wa, w_all.at[0, :, rows(g), :], local_sem.at[1])
    own_wb = pltpu.make_async_copy(wb, w_all.at[1, :, rows(g), :], local_sem.at[2])
    own_feat.start()
    own_wa.start()
    own_wb.start()
    small_all[g] = small[...]
    pool[:, pl.ds(bricks * EDGE, 2 * face + 1)] = jnp.zeros(
        (2, 2 * face + 1, EDGE, EDGE, channels), jnp.float32
    )
    own_feat.wait()
    for j in range(3):
        feat_copy(j).wait()

    def fill(b, carry):
        turned = xt[b].astype(jnp.float32).T
        pool[0, pl.ds(b * EDGE, EDGE)] = turned.reshape(EDGE, EDGE, EDGE, channels)
        return carry

    lax.fori_loop(0, bricks, fill, 0)

    def face_copy(layer, way):
        target = (s + 1, g) if way == 0 else (s - 1, g)
        return remote(
            face_out.at[layer, way], face_in.at[layer, way],
            face_send.at[layer, way], face_recv.at[layer, way], target,
        )

    def send_faces(layer):
        for way, entry, z in ((0, 1, EDGE - 1), (1, 0, 0)):
            for c in range(face):
                slot = jnp.maximum(faces[entry, c], 0)
                chosen = pool[layer, slot * EDGE + z]
                face_out[layer, way, c] = chosen.reshape(PLANE, channels).astype(jnp.bfloat16)

        @pl.when(has_above)
        def _():
            face_copy(layer, 0).start()

        @pl.when(has_below)
        def _():
            face_copy(layer, 1).start()

    def land(layer, way):
        first = bricks * EDGE + way * face
        landed = face_in[layer, way].astype(jnp.float32)
        pool[layer, pl.ds(first, face)] = landed.reshape(face, EDGE, EDGE, channels)

    def receive_faces(layer):
        @pl.when(has_above)
        def _():
            face_copy(layer, 0).wait_send()
            face_copy(layer, 1).wait_recv()
            land(layer, 1)

        @pl.when(has_below)
        def _():
            face_copy(layer, 1).wait_send()
            face_copy(layer, 0).wait_recv()
            land(layer, 0)

    spot = lax.broadcasted_iota(jnp.int32, (EDGE + 2, EDGE, channels), 1)

    def build_plane(layer, b, zp):
        dz = jnp.where(zp == 0, -1, jnp.where(zp == EDGE + 1, 1, 0))
        z = (zp + EDGE - 1) % EDGE

        def strip(dx):
            pieces = []
            for dy in (-1, 0, 1):
                t = table[b, 9 * (dz + 1) + 3 * (dy + 1) + (dx + 1)]
                where = jnp.where(
                    t < 0, blank, jnp.where(t < bricks, t * EDGE + z, bricks * (EDGE - 1) + t)
                )
                got = pool[layer, where]
                pieces.append(got[EDGE - 1 :] if dy < 0 else got if dy == 0 else got[:1])
            return jnp.concatenate(pieces, axis=0)

        left, middle, right = strip(-1), strip(0), strip(1)
        before = pltpu.roll(jnp.where(spot == EDGE - 1, left, middle), 1, 1)
        after = pltpu.roll(jnp.where(spot == 0, right, middle), EDGE - 1, 1)
        for j, value in enumerate((before, middle, after)):
            even[j, b, zp] = value.reshape((EDGE + 2) * EDGE, channels).astype(jnp.bfloat16)
            odd[j, b, zp] = value[1:-1].reshape(PLANE, channels).astype(jnp.bfloat16)

    def build_inner(layer):
        def step(i, carry):
            build_plane(layer, i // EDGE, i % EDGE + 1)
            return carry

        lax.fori_loop(0, bricks * EDGE, step, 0)

    def build_outer(layer):
        def step(b, carry):
            build_plane(layer, b, 0)
            build_plane(layer, b, EDGE + 1)
            return carry

        lax.fori_loop(0, bricks, step, 0)

    def convolve(layer, b):
        acc = None
        for dz in range(3):
            pieces = []
            for dy in range(3):
                for dx in range(3):
                    if dy == 1:
                        piece = odd[dx, b, pl.ds(dz, EDGE)]
                    else:
                        piece = even[dx, b, pl.ds(dz, EDGE), pl.ds(dy * EDGE, PLANE)]
                    pieces.append(piece.reshape(voxels, channels))
            taps = w_all[layer, pl.ds(9 * dz, 9)].reshape(9 * channels, channels)
            part = jnp.dot(
                jnp.concatenate(pieces, axis=1), taps, preferred_element_type=jnp.float32
            )
            acc = part if acc is None else acc + part
        return acc

    def activate(total, b):
        on = jnp.where(table[b, 13] >= 0, 1.0, 0.0)
        return total * (0.5 * on) * (1.0 + jnp.tanh(0.5 * total))

    def gather_weights(layer):
        for part in range(PARTS):
            w_own(layer, part, 0).wait_recv()
            w_forward(layer, part).start()
        for part in range(PARTS):
            w_own(layer, part, 1).wait_recv()
            w_forward(layer, part).wait()
            w_own(layer, part, 0).wait_send()
            w_own(layer, part, 1).wait_send()

    send_faces(0)
    build_inner(0)
    receive_faces(0)
    build_outer(0)
    for j in range(3):
        small_copy(j).wait()
    own_wa.wait()
    gather_weights(0)
    shared = jnp.sum(small_all[...], axis=0)
    row = lax.broadcasted_iota(jnp.int32, shared.shape, 0)
    shift = jnp.sum(jnp.where(row == g, shared, 0.0), axis=0, keepdims=True)
    last = shared[levels : levels + 1]

    def first(b, carry):
        act = activate(convolve(0, b) + shift, b).astype(jnp.bfloat16).astype(jnp.float32)
        pool[1, pl.ds(b * EDGE, EDGE)] = act.reshape(EDGE, EDGE, EDGE, channels)
        return carry

    lax.fori_loop(0, bricks, first, 0)
    send_faces(1)
    build_inner(1)
    receive_faces(1)
    build_outer(1)
    own_wb.wait()
    gather_weights(1)

    def out_copy(b, j):
        return remote(
            staged.at[b, rows(peers[j])], out.at[g, b], out_send.at[b, j], out_recv.at[b, j],
            (s, peers[j]),
        )

    def second(b, carry):
        act = activate(convolve(1, b) + last, b)
        staged[b] = act.T.astype(jnp.bfloat16)
        for j in range(3):
            out_copy(b, j).start()
        out[g, b] = staged[b, rows(g)]
        return carry

    lax.fori_loop(0, bricks, second, 0)

    def finish(b, carry):
        for j in range(3):
            out_copy(b, j).wait()
        return carry

    lax.fori_loop(0, bricks, finish, 0)


def shards(features, neighbours, face_lists, weight_first, bias_first, weight_second, bias_second, level_embed):
    levels, bricks, group, voxels = features.shape
    n_chan = lax.axis_size("chan")
    channels = group * n_chan
    face = face_lists.shape[2]
    rows = jnp.concatenate(
        [bias_first[None] + level_embed, bias_second[None], jnp.zeros((3, group), jnp.float32)]
    )
    lane = lax.broadcasted_iota(jnp.int32, (8, channels), 1)
    small = jnp.where(lane // group == lax.axis_index("chan"), jnp.tile(rows, (1, n_chan)), 0.0)
    planes = bricks * EDGE + 2 * face + 1
    dma = pltpu.SemaphoreType.DMA
    vmem = pl.BlockSpec(memory_space=pltpu.VMEM)
    smem = pl.BlockSpec(memory_space=pltpu.SMEM)
    return pl.pallas_call(
        functools.partial(kernel, lax.axis_size("slab")),
        out_shape=jax.ShapeDtypeStruct(features.shape, features.dtype),
        in_specs=[vmem, smem, smem, vmem, vmem, vmem],
        out_specs=vmem,
        scratch_shapes=[
            pltpu.VMEM((bricks, channels, voxels), jnp.bfloat16),
            pltpu.VMEM((2, 27, channels, channels), jnp.bfloat16),
            pltpu.VMEM((n_chan, 8, channels), jnp.float32),
            pltpu.VMEM((2, planes, EDGE, EDGE, channels), jnp.float32),
            pltpu.VMEM((3, bricks, EDGE + 2, (EDGE + 2) * EDGE, channels), jnp.bfloat16),
            pltpu.VMEM((3, bricks, EDGE + 2, PLANE, channels), jnp.bfloat16),
            pltpu.VMEM((2, 2, face, PLANE, channels), jnp.bfloat16),
            pltpu.VMEM((2, 2, face, PLANE, channels), jnp.bfloat16),
            pltpu.VMEM((bricks, channels, voxels), jnp.bfloat16),
            dma((3,)), dma((3,)),
            dma((2, PARTS, 3)), dma((2, PARTS, 3)),
            dma((3,)), dma((3,)),
            dma((2, 2)), dma((2, 2)),
            dma((bricks, 3)), dma((bricks, 3)),
            dma((3,)),
        ],
        compiler_params=pltpu.CompilerParams(
            collective_id=0, has_side_effects=True, vmem_limit_bytes=48 * 1024 * 1024
        ),
        cost_estimate=pl.CostEstimate(
            flops=4 * 27 * channels * channels * bricks * voxels,
            bytes_accessed=4 * features.size,
            transcendentals=2 * channels * bricks * voxels,
        ),
    )(
        features, neighbours, face_lists[0], small,
        weight_first.transpose(0, 2, 1), weight_second.transpose(0, 2, 1),
    )


def solution(mesh):
    placed = (
        P(None, "slab", "chan", None),
        P("slab", None),
        P("slab", None, None),
        P(None, None, "chan"),
        P("chan"),
        P(None, None, "chan"),
        P("chan"),
        P(None, "chan"),
    )
    return jax.shard_map(
        shards, mesh=mesh, in_specs=placed, out_specs=P(None, "slab", "chan", None), check_vma=False
    )
```

time: 688 us -> 42.5 us (0.06)
  matrix products: 393 us -> 0 us
  waiting for transfers between devices: 119 us -> 0 us
  local copies, waits for them, and re-layouts: 110 us -> 5.88 us
  other arithmetic: 40 us -> 0.09 us
  Pallas kernels: 0 us -> 36.3 us
  between operations: 13.8 us -> 0.04 us
  starting transfers between devices: 10.9 us -> 0 us
    dot_general x216 -> x0, matrix products: 393 us -> none  [shifted_products(): jnp.einsum('oc,cbq->boq', kernel[k], window, preferred_element_type=jnp.f...]
    psum x2 -> x0, waiting for transfers between devices: 106 us -> none  [conv_layer(): whole = lax.psum(term.astype(jnp.bfloat16), 'chan').astype(jnp.float32)]
    gather x8 -> x0, local copies, waits for them, and re-layouts: 62.4 us -> none  [the longest x2 57.1 us: conv_layer(): jnp.take(pool, index.reshape(-1), axis=2)]
    pallas_call x0 -> x1, Pallas kernels: none -> 36.3 us  [shards(): pl.pallas_call(functools.partial(kernel, lax.axis_size('slab')), out_shap...]
    select_n x8 -> x1, other arithmetic: 33.5 us -> 0.01 us  [shards(): jnp.where(lane // group == lax.axis_index('chan'), jnp.tile(rows, (1, n_c...]
    while x10 -> x0, local copies, waits for them, and re-layouts: 15.8 us -> none  [the longest x2 13.4 us: conv_layer(): term = lax.map(per_level, padded)]
    ppermute x4 -> x0, waiting for transfers between devices: 13.8 us -> none  [shifted(): lax.ppermute(value, axis, [(source, source + steps) for source in range(f...]
    ppermute x4 -> x0, starting transfers between devices: 10.9 us -> none  [shifted(): lax.ppermute(value, axis, [(source, source + steps) for source in range(f...]
  transfers between devices with their start and end apart: 6 -> 0, of which waited for: 4 -> 0; matrix products, arithmetic and copies ran while one was open for 1% -> 0% of each run, Pallas kernels for 0% -> 0%
where the time goes in v1:
time: 42.5 us; the launch traced here: 42.3 us
  Pallas kernels  36.3 us (85%)
  local copies, waits for them, and re-layouts  5.88 us (14%)
    pallas_call x1, Pallas kernels, shards(): pl.pallas_call(functools.partial(kernel, lax.axis_size('slab')), out_shap...  36.3 us
    unnamed x17, local copies, waits for them, and re-layouts  5.71 us

profile of v1, /device:TPU:0, one launch (start us, length us, event | category | flops | bytes accessed | tf_op | source)
XLA Modules:
  0.0 42.3 jit_solution(3736474386123893849)
XLA Ops:
  0.0 0.1 pad.2.clone
  0.1 0.0 copy-start.5
  0.1 0.0 copy-start.7
  0.1 0.7 %copy-done.5 = f32[4,32]{1,0:T(4,128)S(1)} copy-done((f32[4,32]{1,0:T(4,128)S(1)}, f32[4,32]{1,0:T(4,128)}, u32[]{:S(2)}) %copy-start.5) | copy-done | bytes 536
  0.8 0.0 copy-done.7
  0.8 0.0 copy-start.6
  0.8 0.7 %copy-done.6 = f32[32]{0:T(128)S(1)} copy-done((f32[32]{0:T(128)S(1)}, f32[32]{0:T(128)}, u32[]{:S(2)}) %copy-start.6) | copy-done | bytes 152
  1.4 0.1 maximum_maximum_fusion
  1.5 0.1 tile.10
  1.6 0.0 copy-start.3
  1.6 0.0 copy-start.4
  1.6 0.7 %copy-done.3 = s32[4,27]{1,0:T(4,128)S(1)} copy-done((s32[4,27]{1,0:T(4,128)S(1)}, s32[4,27]{1,0:T(4,128)}, u32[]{:S(2)}) %copy-start.3) | copy-done | bytes 456
  2.3 0.0 copy-done.4
  2.3 0.0 copy-start
  2.3 1.0 %copy-done = bf16[4,4,32,512]{3,2,1,0:T(8,128)(2,1)S(1)} copy-done((bf16[4,4,32,512]{3,2,1,0:T(8,128)(2,1)S(1)}, bf16[4,4,32,512]{3,2,1,0:T(8,128)(2,1)}, u32[]{:S(2)}) %copy-start) | copy-done | bytes 524312
  3.3 0.0 copy-start.1
  3.3 0.9 %copy-done.1 = bf16[27,128,32]{1,2,0:T(8,128)(2,1)S(1)} copy-done((bf16[27,128,32]{1,2,0:T(8,128)(2,1)S(1)}, bf16[27,128,32]{1,2,0:T(8,128)(2,1)}, u32[]{:S(2)}) %copy-start.1) | copy-done | bytes 221208
  4.3 0.0 copy-start.2
  4.3 0.9 %copy-done.2 = bf16[27,128,32]{1,2,0:T(8,128)(2,1)S(1)} copy-done((bf16[27,128,32]{1,2,0:T(8,128)(2,1)S(1)}, bf16[27,128,32]{1,2,0:T(8,128)(2,1)}, u32[]{:S(2)}) %copy-start.2) | copy-done | bytes 221208
  5.2 36.3 %shard_map.82 = bf16[4,4,32,512]{3,2,1,0:T(8,128)(2,1)S(1)} custom-call(bf16[4,4,32,512]{3,2,1,0:T(8,128)(2,1)S(1)} %copy-done, s32[4,27]{1,0:T(4,128)S(1)} %copy-done.3, s32[2,2]{1,0:T(2,128)S(1)} %bitcast.6, f32[8,128]{1,0:T(8,128)S(1)} %fusion.small, bf16[27,32,128]{2,1,0:T(8,128)(2,1)S(1)} %bitcast.4, bf16[27,32,128]{2,1,0:T(8,128)(2,1)S(1)} %bitcast.5), custom_call_target="tpu_custom_call" | custom-call | flops 3623878656 | bytes 1048576 | tf_op jit(solution)/shard_map/pallas_call | solution.py:295
  41.5 0.8 %copy.10 = bf16[4,4,32,512]{3,2,1,0:T(8,128)(2,1)} copy(bf16[4,4,32,512]{3,2,1,0:T(8,128)(2,1)S(1)} %shard_map.82) | data formatting | bytes 1048576
  (6 shorter events, 0.0 us)
Async XLA Ops:
  0.1 0.7 %copy-start.5 = (f32[4,32]{1,0:T(4,128)S(1)}, f32[4,32]{1,0:T(4,128)}, u32[]{:S(2)}) copy-start(f32[4,32]{1,0:T(4,128)} %param.15) | copy-start | bytes 1540
  0.1 0.7 %copy-start.7 = (f32[32]{0:T(128)S(1)}, f32[32]{0:T(128)}, u32[]{:S(2)}) copy-start(f32[32]{0:T(128)} %param.12) | copy-start | bytes 388
  0.8 0.7 %copy-start.6 = (f32[32]{0:T(128)S(1)}, f32[32]{0:T(128)}, u32[]{:S(2)}) copy-start(f32[32]{0:T(128)} %param.14) | copy-start | bytes 388
  1.6 0.7 %copy-start.3 = (s32[4,27]{1,0:T(4,128)S(1)}, s32[4,27]{1,0:T(4,128)}, u32[]{:S(2)}) copy-start(s32[4,27]{1,0:T(4,128)} %table.1) | copy-start | bytes 1300
  1.6 0.7 %copy-start.4 = (s32[1,2,2]{2,1,0:T(2,128)S(1)}, s32[1,2,2]{2,1,0:T(2,128)}, u32[]{:S(2)}) copy-start(s32[1,2,2]{2,1,0:T(2,128)} %param.10) | copy-start | bytes 52
  2.3 1.0 %copy-start = (bf16[4,4,32,512]{3,2,1,0:T(8,128)(2,1)S(1)}, bf16[4,4,32,512]{3,2,1,0:T(8,128)(2,1)}, u32[]{:S(2)}) copy-start(bf16[4,4,32,512]{3,2,1,0:T(8,128)(2,1)} %feat.1) | copy-start | bytes 1572868
  3.3 0.9 %copy-start.1 = (bf16[27,128,32]{1,2,0:T(8,128)(2,1)S(1)}, bf16[27,128,32]{1,2,0:T(8,128)(2,1)}, u32[]{:S(2)}) copy-start(bf16[27,128,32]{1,2,0:T(8,128)(2,1)} %param.11) | copy-start | bytes 663556
  4.3 0.9 %copy-start.2 = (bf16[27,128,32]{1,2,0:T(8,128)(2,1)S(1)}, bf16[27,128,32]{1,2,0:T(8,128)(2,1)}, u32[]{:S(2)}) copy-start(bf16[27,128,32]{1,2,0:T(8,128)(2,1)} %param.13) | copy-start | bytes 663556

commit v2 on v1

v2 whole, which is shorter than its diff:
```python
import functools

import jax
import jax.numpy as jnp
from jax import lax
from jax.experimental import pallas as pl
from jax.experimental.pallas import tpu as pltpu
from jax.sharding import PartitionSpec as P

MESH = pl.DeviceIdType.MESH
EDGE = 8
PLANE = EDGE * EDGE
PARTS = 3
VMEM_LIMIT = 64 * 1024 * 1024


def kernel(
    slabs,
    feat, table_in, faces_in, first_bias, second_bias, embed, wa, wb,
    out,
    table, faces, first_bias_here, second_bias_here, embed_here, small,
    xt, w_all, small_all, pool, even, odd, acc, face_out, face_in, staged,
    feat_send, feat_recv, w_send, w_recv, small_send, small_recv,
    face_send, face_recv, out_send, out_recv, local_sem, own_sem,
):
    levels, bricks, group, voxels = feat.shape
    face = faces.shape[2]
    channels = xt.shape[1]
    blank = bricks * EDGE
    edges = blank + EDGE
    s, g = lax.axis_index("slab"), lax.axis_index("chan")
    chip, core = g // 2, g % 2
    across = 2 * (1 - chip) + core
    diagonal = 2 * (1 - chip) + (1 - core)
    twin = 2 * chip + (1 - core)
    peers = (across, diagonal, twin)
    has_below, has_above = s > 0, s < slabs - 1

    def rows(owner):
        return pl.ds(pl.multiple_of(owner * group, group), group)

    def local(i, source, target):
        return pltpu.make_async_copy(source, target, local_sem.at[i])

    here = [
        local(0, feat.at[g], xt.at[:, rows(g), :]),
        local(1, first_bias, first_bias_here),
        local(2, second_bias, second_bias_here),
        local(3, embed, embed_here),
        local(4, table_in, table),
        local(5, faces_in, faces),
        local(6, wa, w_all.at[0, :, rows(g), :]),
        local(7, wb, w_all.at[1, :, rows(g), :]),
    ]
    for copy in here:
        copy.start()

    barrier = pltpu.get_barrier_semaphore()
    for peer in peers:
        pl.semaphore_signal(barrier, inc=1, device_id=(s, peer), device_id_type=MESH)

    @pl.when(has_below)
    def _():
        pl.semaphore_signal(barrier, inc=1, device_id=(s - 1, g), device_id_type=MESH)

    @pl.when(has_above)
    def _():
        pl.semaphore_signal(barrier, inc=1, device_id=(s + 1, g), device_id_type=MESH)

    sides = (s + slabs - 1) // slabs + (2 * slabs - 2 - s) // slabs
    pl.semaphore_wait(barrier, len(peers) + sides)

    def remote(src, dst, send, recv, peer):
        return pltpu.make_async_remote_copy(
            src_ref=src, dst_ref=dst, send_sem=send, recv_sem=recv,
            device_id=peer, device_id_type=MESH,
        )

    def feat_copy(b, j):
        return remote(
            feat.at[peers[j], b], xt.at[b, rows(g), :], feat_send.at[b, j], feat_recv.at[b, j],
            (s, peers[j]),
        )

    per = 27 // PARTS

    def w_own(layer, part, j):
        taps = pl.ds(part * per, per)
        source = (wa, wb)[layer]
        return remote(
            source.at[taps], w_all.at[layer, taps, rows(g), :],
            w_send.at[layer, part, j], w_recv.at[layer, part, j],
            (s, (across, twin)[j]),
        )

    def w_forward(layer, part):
        taps = pl.ds(part * per, per)
        block = w_all.at[layer, taps, rows(across), :]
        return remote(
            block, block, w_send.at[layer, part, 2], w_recv.at[layer, part, 2], (s, twin)
        )

    def small_copy(j):
        return remote(
            small, small_all.at[g], small_send.at[j], small_recv.at[j], (s, peers[j])
        )

    def send_weights(layer, parts):
        for part in parts:
            for j in range(2):
                w_own(layer, part, j).start()

    for b in range(bricks):
        for j in range(3):
            feat_copy(b, j).start()
    for i in (1, 2, 3):
        here[i].wait()
    width = first_bias_here.shape[1]
    mine = jnp.concatenate(
        [
            first_bias_here[...] + embed_here[...],
            second_bias_here[...],
            jnp.zeros((7 - levels, width), jnp.float32),
        ],
        axis=0,
    )
    lane = lax.broadcasted_iota(jnp.int32, (8, channels), 1)
    spread = jnp.concatenate([mine] * (channels // width), axis=1)
    small[...] = jnp.where(lane // group == g, spread, 0.0)
    for j in range(3):
        small_copy(j).start()
    small_all[g] = small[...]
    pool[:, pl.ds(blank, EDGE + 2 * face)] = jnp.zeros(
        (2, EDGE + 2 * face, EDGE, EDGE, channels), jnp.float32
    )
    here[0].wait()
    for b in range(bricks):
        for j in range(3):
            feat_copy(b, j).wait_recv()
        turned = xt[b].astype(jnp.float32).T
        pool[0, pl.ds(b * EDGE, EDGE)] = turned.reshape(EDGE, EDGE, EDGE, channels)
        if b == bricks // 2 - 1:
            send_weights(0, (1,))
    send_weights(0, (0, 2))
    for i in (4, 5):
        here[i].wait()

    def face_copy(layer, way):
        target = (s + 1, g) if way == 0 else (s - 1, g)
        return remote(
            face_out.at[layer, way], face_in.at[layer, way],
            face_send.at[layer, way], face_recv.at[layer, way], target,
        )

    def send_faces(layer):
        for way, entry, z in ((0, 1, EDGE - 1), (1, 0, 0)):
            for c in range(face):
                slot = jnp.maximum(faces[0, entry, c], 0)
                chosen = pool[layer, slot * EDGE + z]
                face_out[layer, way, c] = chosen.reshape(PLANE, channels).astype(jnp.bfloat16)

        @pl.when(has_above)
        def _():
            face_copy(layer, 0).start()

        @pl.when(has_below)
        def _():
            face_copy(layer, 1).start()

    def land(layer, way):
        first = edges + way * face
        landed = face_in[layer, way].astype(jnp.float32)
        pool[layer, pl.ds(first, face)] = landed.reshape(face, EDGE, EDGE, channels)

    def receive_faces(layer):
        @pl.when(has_above)
        def _():
            face_copy(layer, 0).wait_send()
            face_copy(layer, 1).wait_recv()
            land(layer, 1)

        @pl.when(has_below)
        def _():
            face_copy(layer, 1).wait_send()
            face_copy(layer, 0).wait_recv()
            land(layer, 0)

    spot = lax.broadcasted_iota(jnp.int32, (EDGE + 2, EDGE, channels), 1)

    def build_plane(layer, b, dz, z):
        def strip(dx):
            pieces = []
            for dy in (-1, 0, 1):
                t = table[b, 9 * (dz + 1) + 3 * (dy + 1) + (dx + 1)]
                place = jnp.where(t < 0, blank, t * EDGE) + z
                if dz != 0:
                    place = jnp.where(t < bricks, place, edges - bricks + t)
                got = pool[layer, place]
                pieces.append(got[EDGE - 1 :] if dy < 0 else got if dy == 0 else got[:1])
            return jnp.concatenate(pieces, axis=0)

        left, middle, right = strip(-1), strip(0), strip(1)
        before = pltpu.roll(jnp.where(spot == EDGE - 1, left, middle), 1, 1)
        after = pltpu.roll(jnp.where(spot == 0, right, middle), EDGE - 1, 1)
        zp = z + 1 + EDGE * dz
        for j, value in enumerate((before, middle, after)):
            even[j, b, zp] = value.reshape((EDGE + 2) * EDGE, channels).astype(jnp.bfloat16)
            odd[j, b, zp] = value[1:-1].reshape(PLANE, channels).astype(jnp.bfloat16)

    def build_inner(layer):
        def step(b, carry):
            for z in range(EDGE):
                build_plane(layer, b, 0, z)
            return carry

        lax.fori_loop(0, bricks, step, 0)

    def build_outer(layer):
        def step(b, carry):
            build_plane(layer, b, -1, EDGE - 1)
            build_plane(layer, b, 1, 0)
            return carry

        lax.fori_loop(0, bricks, step, 0)

    def operand(b, first, count):
        pieces = []
        for dy in range(3):
            for dx in range(3):
                if dy == 1:
                    piece = odd[dx, b, pl.ds(first, count)]
                else:
                    piece = even[dx, b, pl.ds(first, count), pl.ds(dy * EDGE, PLANE)]
                pieces.append(piece.reshape(count * PLANE, channels))
        return jnp.concatenate(pieces, axis=1)

    def taps_of(layer, dz):
        return w_all[layer, pl.ds(9 * dz, 9)].reshape(9 * channels, channels)

    def middle_products(layer):
        def step(b, carry):
            acc[b] = jnp.dot(
                operand(b, 1, EDGE), taps_of(layer, 1), preferred_element_type=jnp.float32
            )
            return carry

        lax.fori_loop(0, bricks, step, 0)

    def convolve(layer, b):
        both = jnp.concatenate([taps_of(layer, 0), taps_of(layer, 2)], axis=1)
        wide = jnp.dot(operand(b, 0, EDGE + 2), both, preferred_element_type=jnp.float32)
        return acc[b] + wide[:voxels, :channels] + wide[2 * PLANE :, channels:]

    def activate(total, b):
        on = jnp.where(table[b, 13] >= 0, 1.0, 0.0)
        return total * (0.5 * on) * (1.0 + jnp.tanh(0.5 * total))

    def gather_weights(layer, parts):
        for part in parts:
            w_own(layer, part, 0).wait_recv()
            w_forward(layer, part).start()
        for part in parts:
            w_own(layer, part, 1).wait_recv()
            w_forward(layer, part).wait()
            w_own(layer, part, 0).wait_send()
            w_own(layer, part, 1).wait_send()

    send_faces(0)
    build_inner(0)
    send_weights(1, (1, 0, 2))
    here[6].wait()
    gather_weights(0, (1,))
    middle_products(0)
    receive_faces(0)
    build_outer(0)
    gather_weights(0, (0, 2))
    for j in range(3):
        small_copy(j).wait()
    shared = jnp.sum(small_all[...], axis=0)
    row = lax.broadcasted_iota(jnp.int32, shared.shape, 0)
    shift = jnp.sum(jnp.where(row == g, shared, 0.0), axis=0, keepdims=True)
    last = shared[levels : levels + 1]

    def first(b, carry):
        act = activate(convolve(0, b) + shift, b).astype(jnp.bfloat16).astype(jnp.float32)
        pool[1, pl.ds(b * EDGE, EDGE)] = act.reshape(EDGE, EDGE, EDGE, channels)
        return carry

    lax.fori_loop(0, bricks, first, 0)
    send_faces(1)
    build_inner(1)
    here[7].wait()
    gather_weights(1, (1, 0, 2))
    middle_products(1)
    receive_faces(1)
    build_outer(1)

    def out_copy(b, j):
        return remote(
            staged.at[b, rows(peers[j])], out.at[g, b], out_send.at[b, j], out_recv.at[b, j],
            (s, peers[j]),
        )

    def out_here(b):
        return pltpu.make_async_copy(staged.at[b, rows(g)], out.at[g, b], own_sem.at[b])

    def second(b, carry):
        act = activate(convolve(1, b) + last, b)
        staged[b] = act.T.astype(jnp.bfloat16)
        for j in range(3):
            out_copy(b, j).start()
        out_here(b).start()
        return carry

    lax.fori_loop(0, bricks, second, 0)

    def finish(b, carry):
        out_here(b).wait()
        for j in range(3):
            out_copy(b, j).wait()
            feat_copy(b, j).wait_send()
        return carry

    lax.fori_loop(0, bricks, finish, 0)


def shards(features, neighbours, face_lists, weight_first, bias_first, weight_second, bias_second, level_embed):
    levels, bricks, group, voxels = features.shape
    n_chan = lax.axis_size("chan")
    channels = group * n_chan
    face = face_lists.shape[2]
    planes = bricks * EDGE + EDGE + 2 * face
    dma = pltpu.SemaphoreType.DMA
    return pl.pallas_call(
        functools.partial(kernel, lax.axis_size("slab")),
        out_shape=jax.ShapeDtypeStruct(features.shape, features.dtype),
        in_specs=[pl.BlockSpec(memory_space=pl.ANY)] * 8,
        out_specs=pl.BlockSpec(memory_space=pl.ANY),
        scratch_shapes=[
            pltpu.SMEM(neighbours.shape, jnp.int32),
            pltpu.SMEM(face_lists.shape, jnp.int32),
            pltpu.VMEM((1, group), jnp.float32),
            pltpu.VMEM((1, group), jnp.float32),
            pltpu.VMEM((levels, group), jnp.float32),
            pltpu.VMEM((8, channels), jnp.float32),
            pltpu.VMEM((bricks, channels, voxels), jnp.bfloat16),
            pltpu.VMEM((2, 27, channels, channels), jnp.bfloat16),
            pltpu.VMEM((n_chan, 8, channels), jnp.float32),
            pltpu.VMEM((2, planes, EDGE, EDGE, channels), jnp.float32),
            pltpu.VMEM((3, bricks, EDGE + 2, (EDGE + 2) * EDGE, channels), jnp.bfloat16),
            pltpu.VMEM((3, bricks, EDGE + 2, PLANE, channels), jnp.bfloat16),
            pltpu.VMEM((bricks, voxels, channels), jnp.float32),
            pltpu.VMEM((2, 2, face, PLANE, channels), jnp.bfloat16),
            pltpu.VMEM((2, 2, face, PLANE, channels), jnp.bfloat16),
            pltpu.VMEM((bricks, channels, voxels), jnp.bfloat16),
            dma((bricks, 3)), dma((bricks, 3)),
            dma((2, PARTS, 3)), dma((2, PARTS, 3)),
            dma((3,)), dma((3,)),
            dma((2, 2)), dma((2, 2)),
            dma((bricks, 3)), dma((bricks, 3)),
            dma((8,)), dma((bricks,)),
        ],
        compiler_params=pltpu.CompilerParams(
            collective_id=0, has_side_effects=True, vmem_limit_bytes=VMEM_LIMIT
        ),
        cost_estimate=pl.CostEstimate(
            flops=4 * 27 * channels * channels * bricks * voxels,
            bytes_accessed=4 * features.size,
            transcendentals=2 * channels * bricks * voxels,
        ),
    )(
        features, neighbours, face_lists, bias_first[None], bias_second[None], level_embed,
        weight_first.transpose(0, 2, 1), weight_second.transpose(0, 2, 1),
    )


def solution(mesh):
    placed = (
        P(None, "slab", "chan", None),
        P("slab", None),
        P("slab", None, None),
        P(None, None, "chan"),
        P("chan"),
        P(None, None, "chan"),
        P("chan"),
        P(None, "chan"),
    )
    return jax.shard_map(
        shards, mesh=mesh, in_specs=placed, out_specs=P(None, "slab", "chan", None), check_vma=False
    )
```

time: 42.5 us -> 35.1 us (0.83)
  local copies, waits for them, and re-layouts: 5.88 us -> 1.88 us
  Pallas kernels: 36.3 us -> 33.1 us
    unnamed x17 -> x1, local copies, waits for them, and re-layouts: 5.71 us -> 1.88 us
    pallas_call x1, Pallas kernels: 36.3 us -> 33.1 us  [shards(): pl.pallas_call(functools.partial(kernel, lax.axis_size('slab')), out_shap...]
where the time goes in v2:
time: 35.1 us; the launch traced here: 35 us
  Pallas kernels  33.1 us (94%)
  local copies, waits for them, and re-layouts  1.88 us (5%)
    pallas_call x1, Pallas kernels, shards(): pl.pallas_call(functools.partial(kernel, lax.axis_size('slab')), out_shap...  33.1 us
    unnamed x1, local copies, waits for them, and re-layouts  1.88 us

profile of v2, /device:TPU:0, one launch (start us, length us, event | category | flops | bytes accessed | tf_op | source)
XLA Modules:
  0.0 35.0 jit_solution(16524432837975782219)
XLA Ops:
  0.0 33.1 %shard_map.82 = bf16[4,4,32,512]{3,2,1,0:T(8,128)(2,1)} custom-call(bf16[4,4,32,512]{3,2,1,0:T(8,128)(2,1)} %feat.1, s32[4,27]{1,0:T(4,128)} %table_in.1, s32[1,2,2]{2,1,0:T(2,128)} %faces_in.1, f32[1,32]{1,0:T(1,128)} %bitcast.6, f32[1,32]{1,0:T(1,128)} %bitcast.7, f32[4,32]{1,0:T(4,128)} %embed.1, bf16[27,32,128]{2,1,0:T(8,128)(2,1)} %bitcast.4, ...), custom_call_target="tpu_custom_call" | custom-call | flops 3623878656 | bytes 1048576 | tf_op jit(solution)/shard_map/pallas_call | solution.py:334
  33.1 1.9 %copy.10 = bf16[4,4,32,512]{3,2,1,0:T(8,128)(2,1)} copy(bf16[4,4,32,512]{3,2,1,0:T(8,128)(2,1)} %shard_map.82) | data formatting | bytes 1048576

commit v3 on v2

--- a/solution.py
+++ b/solution.py
@@ -11,7 +11,9 @@
 EDGE = 8
 PLANE = EDGE * EDGE
 PARTS = 3
-VMEM_LIMIT = 64 * 1024 * 1024
+LANES = 128
+ORDER = (0, 3, 1, 2)
+VMEM_LIMIT = 63 * 1024 * 1024
 
 
 def kernel(
@@ -76,10 +78,11 @@
             device_id=peer, device_id_type=MESH,
         )
 
-    def feat_copy(b, j):
-        return remote(
-            feat.at[peers[j], b], xt.at[b, rows(g), :], feat_send.at[b, j], feat_recv.at[b, j],
-            (s, peers[j]),
+    def feat_copy(q, j):
+        part = pl.ds(q * LANES, LANES)
+        return remote(
+            feat.at[peers[j], :, :, part], xt.at[:, rows(g), part],
+            feat_send.at[q, j], feat_recv.at[q, j], (s, peers[j]),
         )
 
     per = 27 // PARTS
@@ -110,9 +113,9 @@
             for j in range(2):
                 w_own(layer, part, j).start()
 
-    for b in range(bricks):
-        for j in range(3):
-            feat_copy(b, j).start()
+    for q in ORDER:
+        for j in range(3):
+            feat_copy(q, j).start()
     for i in (1, 2, 3):
         here[i].wait()
     width = first_bias_here.shape[1]
@@ -133,18 +136,6 @@
     pool[:, pl.ds(blank, EDGE + 2 * face)] = jnp.zeros(
         (2, EDGE + 2 * face, EDGE, EDGE, channels), jnp.float32
     )
-    here[0].wait()
-    for b in range(bricks):
-        for j in range(3):
-            feat_copy(b, j).wait_recv()
-        turned = xt[b].astype(jnp.float32).T
-        pool[0, pl.ds(b * EDGE, EDGE)] = turned.reshape(EDGE, EDGE, EDGE, channels)
-        if b == bricks // 2 - 1:
-            send_weights(0, (1,))
-    send_weights(0, (0, 2))
-    for i in (4, 5):
-        here[i].wait()
-
     def face_copy(layer, way):
         target = (s + 1, g) if way == 0 else (s - 1, g)
         return remote(
@@ -207,21 +198,17 @@
             even[j, b, zp] = value.reshape((EDGE + 2) * EDGE, channels).astype(jnp.bfloat16)
             odd[j, b, zp] = value[1:-1].reshape(PLANE, channels).astype(jnp.bfloat16)
 
-    def build_inner(layer):
+    def build_inner(layer, first, count):
         def step(b, carry):
-            for z in range(EDGE):
+            for z in range(first, first + count):
                 build_plane(layer, b, 0, z)
             return carry
 
         lax.fori_loop(0, bricks, step, 0)
 
-    def build_outer(layer):
-        def step(b, carry):
-            build_plane(layer, b, -1, EDGE - 1)
-            build_plane(layer, b, 1, 0)
-            return carry
-
-        lax.fori_loop(0, bricks, step, 0)
+    def build_outer(layer, b):
+        build_plane(layer, b, -1, EDGE - 1)
+        build_plane(layer, b, 1, 0)
 
     def operand(b, first, count):
         pieces = []
@@ -237,19 +224,15 @@
     def taps_of(layer, dz):
         return w_all[layer, pl.ds(9 * dz, 9)].reshape(9 * channels, channels)
 
-    def middle_products(layer):
-        def step(b, carry):
-            acc[b] = jnp.dot(
-                operand(b, 1, EDGE), taps_of(layer, 1), preferred_element_type=jnp.float32
-            )
-            return carry
-
-        lax.fori_loop(0, bricks, step, 0)
-
-    def convolve(layer, b):
+    def middle(layer, b):
+        return jnp.dot(
+            operand(b, 1, EDGE), taps_of(layer, 1), preferred_element_type=jnp.float32
+        )
+
+    def outer(layer, b):
         both = jnp.concatenate([taps_of(layer, 0), taps_of(layer, 2)], axis=1)
         wide = jnp.dot(operand(b, 0, EDGE + 2), both, preferred_element_type=jnp.float32)
-        return acc[b] + wide[:voxels, :channels] + wide[2 * PLANE :, channels:]
+        return wide[:voxels, :channels] + wide[2 * PLANE :, channels:]
 
     def activate(total, b):
         on = jnp.where(table[b, 13] >= 0, 1.0, 0.0)
@@ -265,14 +248,37 @@
             w_own(layer, part, 0).wait_send()
             w_own(layer, part, 1).wait_send()
 
-    send_faces(0)
-    build_inner(0)
+    for i in (0, 4, 5):
+        here[i].wait()
+    deep = LANES // PLANE
+    for i, q in enumerate(ORDER):
+        for j in range(3):
+            feat_copy(q, j).wait_recv()
+        if i == 2:
+            send_weights(0, (1,))
+        if i == 3:
+            send_weights(0, (0, 2))
+
+        def fill(b, carry):
+            turned = xt[b, :, pl.ds(q * LANES, LANES)].astype(jnp.float32).T
+            pool[0, pl.ds(b * EDGE + q * deep, deep)] = turned.reshape(deep, EDGE, EDGE, channels)
+            return carry
+
+        lax.fori_loop(0, bricks, fill, 0)
+        if i == 1:
+            send_faces(0)
+        build_inner(0, q * deep, deep)
     send_weights(1, (1, 0, 2))
+    receive_faces(0)
     here[6].wait()
     gather_weights(0, (1,))
-    middle_products(0)
-    receive_faces(0)
-    build_outer(0)
+
+    def begin(b, carry):
+        acc[b] = middle(0, b)
+        build_outer(0, b)
+        return carry
+
+    lax.fori_loop(0, bricks, begin, 0)
     gather_weights(0, (0, 2))
     for j in range(3):
         small_copy(j).wait()
@@ -282,18 +288,16 @@
     last = shared[levels : levels + 1]
 
     def first(b, carry):
-        act = activate(convolve(0, b) + shift, b).astype(jnp.bfloat16).astype(jnp.float32)
+        act = activate(acc[b] + outer(0, b) + shift, b).astype(jnp.bfloat16).astype(jnp.float32)
         pool[1, pl.ds(b * EDGE, EDGE)] = act.reshape(EDGE, EDGE, EDGE, channels)
         return carry
 
     lax.fori_loop(0, bricks, first, 0)
     send_faces(1)
-    build_inner(1)
+    build_inner(1, 0, EDGE)
     here[7].wait()
     gather_weights(1, (1, 0, 2))
-    middle_products(1)
     receive_faces(1)
-    build_outer(1)
 
     def out_copy(b, j):
         return remote(
@@ -305,7 +309,9 @@
         return pltpu.make_async_copy(staged.at[b, rows(g)], out.at[g, b], own_sem.at[b])
 
     def second(b, carry):
-        act = activate(convolve(1, b) + last, b)
+        centre = middle(1, b)
+        build_outer(1, b)
+        act = activate(centre + outer(1, b) + last, b)
         staged[b] = act.T.astype(jnp.bfloat16)
         for j in range(3):
             out_copy(b, j).start()
@@ -318,10 +324,12 @@
         out_here(b).wait()
         for j in range(3):
             out_copy(b, j).wait()
-            feat_copy(b, j).wait_send()
         return carry
 
     lax.fori_loop(0, bricks, finish, 0)
+    for q in ORDER:
+        for j in range(3):
+            feat_copy(q, j).wait_send()
 
 
 def shards(features, neighbours, face_lists, weight_first, bias_first, weight_second, bias_second, level_embed):
@@ -333,7 +341,7 @@
     dma = pltpu.SemaphoreType.DMA
     return pl.pallas_call(
         functools.partial(kernel, lax.axis_size("slab")),
-        out_shape=jax.ShapeDtypeStruct(features.shape, features.dtype),
+        out_shape=pltpu.VMEM(features.shape, features.dtype),
         in_specs=[pl.BlockSpec(memory_space=pl.ANY)] * 8,
         out_specs=pl.BlockSpec(memory_space=pl.ANY),
         scratch_shapes=[
@@ -353,7 +361,7 @@
             pltpu.VMEM((2, 2, face, PLANE, channels), jnp.bfloat16),
             pltpu.VMEM((2, 2, face, PLANE, channels), jnp.bfloat16),
             pltpu.VMEM((bricks, channels, voxels), jnp.bfloat16),
-            dma((bricks, 3)), dma((bricks, 3)),
+            dma((4, 3)), dma((4, 3)),
             dma((2, PARTS, 3)), dma((2, PARTS, 3)),
             dma((3,)), dma((3,)),
             dma((2, 2)), dma((2, 2)),

time: 35.1 us -> 34.1 us (0.972)
  local copies, waits for them, and re-layouts: 1.88 us -> 0.8 us
    unnamed x1, local copies, waits for them, and re-layouts: 1.88 us -> 0.8 us
where the time goes in v3:
time: 34.1 us; the launch traced here: 33.9 us
  Pallas kernels  33.1 us (97%)
  local copies, waits for them, and re-layouts  0.8 us (2%)
    pallas_call x1, Pallas kernels, shards(): pl.pallas_call(functools.partial(kernel, lax.axis_size('slab')), out_shap...  33.1 us
    unnamed x1, local copies, waits for them, and re-layouts  0.8 us

profile of v3, /device:TPU:0, one launch (start us, length us, event | category | flops | bytes accessed | tf_op | source)
XLA Modules:
  0.0 33.9 jit_solution(1983099225896131130)
XLA Ops:
  0.0 33.1 %shard_map.82 = bf16[4,4,32,512]{3,2,1,0:T(8,128)(2,1)S(1)} custom-call(bf16[4,4,32,512]{3,2,1,0:T(8,128)(2,1)} %feat.1, s32[4,27]{1,0:T(4,128)} %table_in.1, s32[1,2,2]{2,1,0:T(2,128)} %faces_in.1, f32[1,32]{1,0:T(1,128)} %bitcast.6, f32[1,32]{1,0:T(1,128)} %bitcast.7, f32[4,32]{1,0:T(4,128)} %embed.1, bf16[27,32,128]{2,1,0:T(8,128)(2,1)} %bitcast.4, ...), custom_call_target="tpu_custom_call" | custom-call | flops 3623878656 | bytes 1048576 | tf_op jit(solution)/shard_map/pallas_call | solution.py:342
  33.1 0.8 %copy.10 = bf16[4,4,32,512]{3,2,1,0:T(8,128)(2,1)} copy(bf16[4,4,32,512]{3,2,1,0:T(8,128)(2,1)S(1)} %shard_map.82) | data formatting | bytes 1048576
